TPU v7x, 1024 devices: a whole 4x4x32 slice. The times are simulated.
1024 devices in a mesh: dp: 32 (over y, z_hi, core), tensor: 32 (over z_lo, x).
Axes of the slice: x: 4, y: 4, z: 32 (z_hi: 4, z_lo: 8; z = z_hi * 8 + z_lo), core: 2. Of those that a mesh axis runs over, the one named last changes fastest.
Arguments:
- out_grad: bfloat16 [12288, 5120], P(('dp', 'tensor')), may hold values from -24 to 24
- gate_pre: bfloat16 [12288, 14336], P('dp', 'tensor'), may hold values from -6 to 6
- up_pre: bfloat16 [12288, 14336], P('dp', 'tensor'), may hold values from -6 to 6
- down_weight: bfloat16 [14336, 5120], P('tensor'), may hold values from -0.078125 to 0.078125
Outputs:
- gate_grad: bfloat16 [12288, 14336], P('dp', 'tensor')
- up_grad: bfloat16 [12288, 14336], P('dp', 'tensor')
- weight_grad: float32 [14336, 5120], P('tensor', 'dp')
All inputs are finite; a program needn't handle non-finite values.
Results may differ from a plain program's by a relative error of at most 0.018.
Values may be sent and summed in bfloat16 or wider, within the bound.
A program may use at most 64 MiB of HBM per device.

v0:
```python
import jax
import jax.numpy as jnp
from jax import lax
from jax.sharding import PartitionSpec as P


def per_device(out_grad, gate_pre, up_pre, down_weight):
    rows_all = lax.all_gather(out_grad, "tensor", axis=0, tiled=True)
    gate_wide = gate_pre.astype(jnp.float32)
    up_wide = up_pre.astype(jnp.float32)
    logistic = jax.nn.sigmoid(gate_wide)
    swish = gate_wide * logistic
    hidden = (swish * up_wide).astype(jnp.bfloat16)
    back_grad = lax.dot_general(
        rows_all, down_weight, (((1,), (1,)), ((), ())), preferred_element_type=jnp.float32
    )
    up_grad = (back_grad * swish).astype(jnp.bfloat16)
    gate_grad = (back_grad * up_wide * logistic * (1.0 + gate_wide * (1.0 - logistic))).astype(
        jnp.bfloat16
    )
    factor = float(gate_pre.shape[0] * lax.axis_size("dp")) ** (-0.5)
    partial_value = lax.dot_general(
        hidden, rows_all, (((0,), (0,)), ((), ())), preferred_element_type=jnp.float32
    )
    shared = lax.psum_scatter(
        partial_value.astype(jnp.bfloat16), "dp", scatter_dimension=1, tiled=True
    ).astype(jnp.float32)
    weight_grad = shared * jnp.float32(factor)
    return (gate_grad, up_grad, weight_grad)


def solution(mesh):
    placed = (P(("dp", "tensor"), None), P("dp", "tensor"), P("dp", "tensor"), P("tensor", None))
    return jax.shard_map(
        per_device,
        mesh=mesh,
        in_specs=placed,
        out_specs=(P("dp", "tensor"), P("dp", "tensor"), P("tensor", "dp")),
        check_vma=False,
    )
```

profile of v0, /device:TPU:1, one launch (start us, length us, event | category | flops | bytes accessed | tf_op | source)
XLA Modules:
  0.0 524.5 jit_solution(3875710416303244098)
XLA Ops:
  7.2 0.0 all-gather.3.cloned.1.call-start
  7.2 0.7 all-gather.3.cloned.1.call-update
  7.9 0.0 copy-start
  7.9 0.0 copy-start.1
  7.9 0.0 reduce-scatter.2.cloned.1.call-start
  8.0 233.0 %all-gather.3.cloned.1.call-done = bf16[32,12,5120]{2,1,0:T(8,128)(2,1)} async-done(((bf16[1,12,5120]{2,1,0:T(8,128)(2,1)}), bf16[32,12,5120]{2,1,0:T(8,128)(2,1)}) %all-gather.3.cloned.1.call-update) | async-done | bytes 3932176 | tf_op jit(solution)/shard_map/all_gather | solution.py:8
  241.0 7.1 %reshape.7 = bf16[384,5120]{1,0:T(8,128)(2,1)} reshape(bf16[32,12,5120]{2,1,0:T(8,128)(2,1)} %all-gather.3.cloned.1.call-done) | data formatting | bytes 7864320
  248.1 0.0 copy-done
  248.1 0.0 copy-done.1
  248.1 7.5 %convolution_convert_fusion = bf16[448,5120]{0,1:T(8,128)(2,1)} fusion(bf16[384,5120]{1,0:T(8,128)(2,1)} %reshape.7, bf16[384,448]{0,1:T(8,128)(2,1)S(1)} %copy-done.1, bf16[384,448]{0,1:T(8,128)(2,1)S(1)} %copy-done), kind=kOutput, calls=%fused_computation | convolution fusion | flops 1765277696 | bytes 9207808 | tf_op jit(solution)/shard_map/dot_general | solution.py:22
  255.5 0.0 reduce-scatter.2.cloned.1.call-update
  255.6 7.0 %multiply_convert_fusion = (bf16[384,448]{0,1:T(8,128)(2,1)}, bf16[384,448]{0,1:T(8,128)(2,1)}) fusion(bf16[384,448]{0,1:T(8,128)(2,1)S(1)} %copy-done, bf16[384,448]{0,1:T(8,128)(2,1)S(1)} %copy-done.1, bf16[384,5120]{1,0:T(8,128)(2,1)} %reshape.7, bf16[448,5120]{1,0:T(8,128)(2,1)} %param.7), kind=kOutput, calls=%fused_computation.14 | convolution fusion | flops 1764188160 | bytes 9895936 | tf_op jit(solution)/shard_map/dot_general | solution.py:14
  262.6 253.4 %reduce-scatter.2.cloned.1.call-done = bf16[448,160]{0,1:T(8,128)(2,1)} async-done(((bf16[448,5120]{0,1:T(8,128)(2,1)}), bf16[448,160]{0,1:T(8,128)(2,1)}) %reduce-scatter.2.cloned.1.call-update) | async-done | bytes 143376 | tf_op jit(solution)/shard_map/reduce_scatter | solution.py:25
  515.9 1.7 convert_multiply_fusion.4
Async XLA Ops:
  7.2 233.8 %all-gather.3.cloned.1.call-start = ((), (), s32[]{:S(2)}) async-start(), calls=%async_computation.2 | async-start | bytes 5406720 | tf_op jit(solution)/shard_map/all_gather | solution.py:8
  7.9 240.2 %copy-start = (bf16[384,448]{0,1:T(8,128)(2,1)S(1)}, bf16[384,448]{0,1:T(8,128)(2,1)}, u32[]{:S(2)}) copy-start(bf16[384,448]{0,1:T(8,128)(2,1)} %param.5) | copy-start | bytes 1032196
  7.9 240.2 %copy-start.1 = (bf16[384,448]{0,1:T(8,128)(2,1)S(1)}, bf16[384,448]{0,1:T(8,128)(2,1)}, u32[]{:S(2)}) copy-start(bf16[384,448]{0,1:T(8,128)(2,1)} %param.6) | copy-start | bytes 1032196
  7.9 508.0 %reduce-scatter.2.cloned.1.call-start = ((), (), s32[]{:S(2)}) async-start(), calls=%async_computation.1 | async-start | bytes 5406720 | tf_op jit(solution)/shard_map/reduce_scatter | solution.py:25
Sparse Core Ops, SparseCore 0:
  10.7 230.2 all-gather.2
  255.7 260.2 reduce-scatter.1
where the time goes:
time: 525 us; the launch traced here: 524 us
  waiting for transfers between devices  487 us (93%)
  matrix products  14.5 us (3%)
  between operations  14.1 us (3%)
  local copies, waits for them, and re-layouts  7.12 us (1%)
    reduce_scatter x1, waiting for transfers between devices, per_device(): lax.psum_scatter(partial_value.astype(jnp.bfloat16), 'dp', scatter_dimens...  253 us
    all_gather x1, waiting for transfers between devices, per_device(): rows_all = lax.all_gather(out_grad, 'tensor', axis=0, tiled=True)  233 us
  transfers between devices with their start and end apart: 2, of which 2 were waited for; matrix products, arithmetic and copies ran while one was open for 1% of the time, Pallas kernels for 0%

commit v1 on v0

v1 whole, which is shorter than its diff:
```python
import functools

import jax
import jax.numpy as jnp
from jax import lax
from jax.experimental import pallas as pl
from jax.experimental.pallas import tpu as pltpu
from jax.sharding import PartitionSpec as P

MESH = pl.DeviceIdType.MESH
BF = jnp.bfloat16
F32 = jnp.float32

NX = 4
NZ = 8
NK = 5
TOK = 384
OWN = 12
LINE = 48
FFL = 448
HALF = 224
QUARTER = 1280
WIDE = 160
R0 = 64
RR = 112


def tile_columns(load, k):
    sides = []
    for c in range(2):
        if k < 4:
            at = k * 2 * WIDE + c * WIDE
            sides.append(load(at, 128))
        else:
            sides.append(
                jnp.concatenate([load(z * 2 * WIDE + c * WIDE + 128, 32) for z in range(4)], axis=1)
            )
    return sides


def kernel(
    og, gate_hbm, up_hbm, w_hbm,
    gg, ug, wg,
    gate, up, w, wp, ht, xs, asend, arecv, bg, pm, csend, crecv,
    y1s, y1r, y2s, y2r, z1s, z1r, z2s, z2r, zf, pr, q1s, q1r, q2s, q2r,
    lsem, a_s, a_r, l_s, l_r, x_s, x_r, c_s, c_r, y_s, y_r, z_s, z_r,
):
    dp = lax.axis_index("dp")
    tn = lax.axis_index("tensor")
    y, zh, core = dp // 8, (dp // 2) % 4, dp % 2
    zl, x = tn // 4, tn % 4

    def at_x(d):
        return (dp, zl * 4 + (x + d) % 4)

    def at_y(d):
        return (((y + d) % 4) * 8 + zh * 2 + core, tn)

    def at_z(d):
        return (y * 8 + ((zh + d) % 4) * 2 + core, tn)

    def at_line(d):
        return (dp, tn + 4 * d)

    other = (dp + 1 - 2 * core, tn)

    loads = [
        pltpu.make_async_copy(gate_hbm, gate, lsem.at[0]),
        pltpu.make_async_copy(up_hbm, up, lsem.at[1]),
        pltpu.make_async_copy(w_hbm, w, lsem.at[2]),
    ]
    for copy in loads:
        copy.start()

    barrier = pltpu.get_barrier_semaphore()

    def greet(device):
        pl.semaphore_signal(barrier, inc=1, device_id=device, device_id_type=MESH)

    for device in (at_x(1), at_x(2), at_x(3), other, at_y(1), at_y(3), at_z(1), at_z(3)):
        greet(device)

    @pl.when(zl > 0)
    def _():
        greet(at_line(-1))

    @pl.when(zl < NZ - 1)
    def _():
        greet(at_line(1))

    asend[...] = jnp.zeros_like(asend)
    for q in range(4):
        for k in range(NK):
            lo, hi = tile_columns(lambda at, n: og[:, q * QUARTER + at : q * QUARTER + at + n], k)
            asend[q, k, 0:OWN, 0:128] = lo
            asend[q, k, 0:OWN, 128:256] = hi
    inner = jnp.where(zl > 0, 1, 0) + jnp.where(zl < NZ - 1, 1, 0)
    pl.semaphore_wait(barrier, 8 + inner)

    drains = []

    def remote(src, dst, ss, rs, device):
        return pltpu.make_async_remote_copy(
            src_ref=src, dst_ref=dst, send_sem=ss, recv_sem=rs, device_id=device, device_id_type=MESH
        )

    def send(src, dst, ss, rs, device):
        copy = remote(src, dst, ss, rs, device)
        copy.start()
        drains.append(copy)

    def arrived(dst, rs):
        remote(dst, dst, rs, rs, other).wait_recv()

    for d in (2, 1, 3):
        send(asend.at[(x + d) % 4], arecv.at[x], a_s.at[d], a_r.at[d], at_x(d))
    arecv[pl.ds(x, 1)] = asend[pl.ds(x, 1)]

    loads[0].wait()
    loads[1].wait()
    g = gate[...].astype(F32)
    hidden = (g * jax.nn.sigmoid(g) * up[...].astype(F32)).astype(BF)
    ht[...] = hidden.T
    for d in (1, 3, 2):
        arrived(arecv.at[(x + 4 - d) % 4], a_r.at[d])

    order = [(zh + 2) % 4, (zh + 1) % 4, (zh + 3) % 4, 4, zh]

    def rows_of(p):
        return pl.ds(pl.multiple_of(p * LINE, 16), LINE)

    for j in range(NK):
        mine = jnp.concatenate([arecv[s, order[j], 0:OWN, :] for s in range(4)], axis=0)
        xs[x, j, rows_of(zl), :] = mine

    def line_copy(j, side, t):
        step = 1 if side == 0 else -1
        block = xs.at[x, j, rows_of(zl - step * (t - 1))]
        return remote(block, block, l_s.at[side, j, t], l_r.at[side, j, t], at_line(step))

    def line_sends(side, t):
        if side == 0:
            return jnp.logical_and(zl - (t - 1) >= 0, zl < NZ - 1)
        return jnp.logical_and(zl + (t - 1) <= NZ - 1, zl > 0)

    def line_gets(side, t):
        return zl - t >= 0 if side == 0 else zl + t <= NZ - 1

    def wave(w_at):
        for j in range(NK):
            t = w_at - 2 * j
            if t < 0 or t > NZ - 1:
                continue
            for side in range(2):
                if t >= 1:
                    @pl.when(line_gets(side, t))
                    def _():
                        step = 1 if side == 0 else -1
                        arrived(xs.at[x, j, rows_of(zl - step * t)], l_r.at[side, j, t])

                if t + 1 <= NZ - 1:
                    @pl.when(line_sends(side, t + 1))
                    def _():
                        line_copy(j, side, t + 1).start()

    def permute(q):
        if q == 0:
            loads[2].wait()
        for k in range(NK):
            lo, hi = tile_columns(lambda at, n: w[:, q * QUARTER + at : q * QUARTER + at + n], k)
            wp[q, k, :, 0:128] = lo
            wp[q, k, :, 128:256] = hi

    def partial(q, j):
        value = jnp.dot(ht[...], xs[q, j], preferred_element_type=F32)
        lo, hi = value[:, 0:128], value[:, 128:256]
        pm[q, j] = jnp.where(core == 0, lo, hi)
        csend[q, j] = jnp.where(core == 0, hi, lo).astype(BF)
        send(csend.at[q, j], crecv.at[q, j], c_s.at[q, j], c_r.at[q, j], other)

    left, right, far = (x + 3) % 4, (x + 1) % 4, (x + 2) % 4
    up_half, down_half = pl.ds(0, TOK // 2), pl.ds(TOK // 2, TOK // 2)

    def op_a(j):
        block = xs.at[x, j]
        send(block, block, x_s.at[0, j], x_r.at[0, j], at_x(1))
        send(block, block, x_s.at[1, j], x_r.at[1, j], at_x(3))
        partial(x, j)

    def op_d(j):
        arrived(xs.at[left, j], x_r.at[0, j])
        block = xs.at[left, j, up_half]
        send(block, block, x_s.at[2, j], x_r.at[2, j], at_x(1))
        arrived(xs.at[right, j], x_r.at[1, j])
        block = xs.at[right, j, down_half]
        send(block, block, x_s.at[3, j], x_r.at[3, j], at_x(3))
        partial(left, j)
        partial(right, j)

    def op_e(j):
        arrived(xs.at[far, j, up_half], x_r.at[2, j])
        arrived(xs.at[far, j, down_half], x_r.at[3, j])
        partial(far, j)

    lo_r, hi_r = pl.ds(0, HALF), pl.ds(HALF, HALF)
    y_far, y_next, y_prev = (y + 2) % 4, (y + 1) % 4, (y + 3) % 4

    def op_f(j):
        for q in range(4):
            arrived(crecv.at[q, j], c_r.at[q, j])
        y1s[j] = (pm[y_far, j] + crecv[y_far, j].astype(F32)).astype(BF)
        send(y1s.at[j, lo_r], y1r.at[j, lo_r], y_s.at[0, j], y_r.at[0, j], at_y(1))
        send(y1s.at[j, hi_r], y1r.at[j, hi_r], y_s.at[1, j], y_r.at[1, j], at_y(3))
        y2s[0, j, hi_r] = (pm[y_next, j, hi_r] + crecv[y_next, j, hi_r].astype(F32)).astype(BF)
        send(y2s.at[0, j, hi_r], y2r.at[0, j, hi_r], y_s.at[2, j], y_r.at[2, j], at_y(1))
        y2s[1, j, lo_r] = (pm[y_prev, j, lo_r] + crecv[y_prev, j, lo_r].astype(F32)).astype(BF)
        send(y2s.at[1, j, lo_r], y2r.at[1, j, lo_r], y_s.at[3, j], y_r.at[3, j], at_y(3))

    def op_g(j):
        arrived(y1r.at[j, lo_r], y_r.at[0, j])
        y2s[0, j, lo_r] = (
            pm[y_next, j, lo_r] + crecv[y_next, j, lo_r].astype(F32) + y1r[j, lo_r].astype(F32)
        ).astype(BF)
        send(y2s.at[0, j, lo_r], y2r.at[0, j, lo_r], y_s.at[4, j], y_r.at[4, j], at_y(1))
        arrived(y1r.at[j, hi_r], y_r.at[1, j])
        y2s[1, j, hi_r] = (
            pm[y_prev, j, hi_r] + crecv[y_prev, j, hi_r].astype(F32) + y1r[j, hi_r].astype(F32)
        ).astype(BF)
        send(y2s.at[1, j, hi_r], y2r.at[1, j, hi_r], y_s.at[5, j], y_r.at[5, j], at_y(3))

    def reduced(j):
        arrived(y2r.at[0, j, hi_r], y_r.at[2, j])
        arrived(y2r.at[1, j, lo_r], y_r.at[3, j])
        arrived(y2r.at[0, j, lo_r], y_r.at[4, j])
        arrived(y2r.at[1, j, hi_r], y_r.at[5, j])
        return (
            pm[y, j] + crecv[y, j].astype(F32) + y2r[0, j].astype(F32) + y2r[1, j].astype(F32)
        )

    z_far, z_next, z_prev = (zh + 2) % 4, (zh + 1) % 4, (zh + 3) % 4

    def op_h(j):
        total = reduced(j)
        if j == 0:
            z1s[...] = total.astype(BF)
            send(z1s.at[lo_r], z1r.at[lo_r], z_s.at[0], z_r.at[0], at_z(1))
            send(z1s.at[hi_r], z1r.at[hi_r], z_s.at[1], z_r.at[1], at_z(3))
        elif j == 1:
            zf[0] = total
            z2s[0, hi_r] = total[HALF:].astype(BF)
            send(z2s.at[0, hi_r], z2r.at[0, hi_r], z_s.at[2], z_r.at[2], at_z(1))
        elif j == 2:
            zf[1] = total
            z2s[1, lo_r] = total[:HALF].astype(BF)
            send(z2s.at[1, lo_r], z2r.at[1, lo_r], z_s.at[3], z_r.at[3], at_z(3))
        elif j == 3:
            for o in range(4):
                pr[o] = jnp.concatenate(
                    [total[RR * n : RR * n + RR, 32 * o : 32 * o + 32] for n in range(4)], axis=1
                )
            q1s[...] = pr[z_far].astype(BF)
            send(q1s.at[c0], q1r.at[c0], z_s.at[6], z_r.at[6], at_z(1))
            send(q1s.at[c1], q1r.at[c1], z_s.at[7], z_r.at[7], at_z(3))
            q2s[0, c1] = pr[z_next, c1].astype(BF)
            send(q2s.at[0, c1], q2r.at[0, c1], z_s.at[8], z_r.at[8], at_z(1))
            q2s[1, c0] = pr[z_prev, c0].astype(BF)
            send(q2s.at[1, c0], q2r.at[1, c0], z_s.at[9], z_r.at[9], at_z(3))
        else:
            zf[2] = total

    c0, c1 = pl.ds(0, R0), pl.ds(R0, RR - R0)

    def z_clockwise():
        arrived(z1r.at[lo_r], z_r.at[0])
        z2s[0, lo_r] = (zf[0, lo_r] + z1r[lo_r].astype(F32)).astype(BF)
        send(z2s.at[0, lo_r], z2r.at[0, lo_r], z_s.at[4], z_r.at[4], at_z(1))

    def z_back():
        arrived(z1r.at[hi_r], z_r.at[1])
        z2s[1, hi_r] = (zf[1, hi_r] + z1r[hi_r].astype(F32)).astype(BF)
        send(z2s.at[1, hi_r], z2r.at[1, hi_r], z_s.at[5], z_r.at[5], at_z(3))

    def z_rest():
        arrived(q1r.at[c0], z_r.at[6])
        q2s[0, c0] = (pr[z_next, c0] + q1r[c0].astype(F32)).astype(BF)
        send(q2s.at[0, c0], q2r.at[0, c0], z_s.at[10], z_r.at[10], at_z(1))
        arrived(q1r.at[c1], z_r.at[7])
        q2s[1, c1] = (pr[z_prev, c1] + q1r[c1].astype(F32)).astype(BF)
        send(q2s.at[1, c1], q2r.at[1, c1], z_s.at[11], z_r.at[11], at_z(3))

    def back(j):
        value = None
        for q in range(4):
            term = lax.dot_general(
                xs[q, j], wp[q, order[j]], (((1,), (1,)), ((), ())), preferred_element_type=F32
            )
            value = term if value is None else value + term
        if j == 0:
            bg[...] = value
        else:
            bg[...] += value

    wave(0)
    for n in range(4):
        wave(n + 1)
        permute(n)
    wave(5)
    wave(6)
    wave(7)
    op_a(0)
    wave(8)
    wave(9)
    wave(10)
    op_d(0)
    op_a(1)
    wave(11)
    op_a(2)
    wave(12)
    op_e(0)
    wave(13)
    op_f(0)
    op_d(1)
    wave(14)
    op_a(3)
    op_g(0)
    wave(15)
    op_e(1)
    op_h(0)
    op_f(1)
    op_d(2)
    op_a(4)
    op_g(1)
    op_e(2)
    op_h(1)
    op_f(2)
    op_d(3)
    op_g(2)
    op_e(3)
    op_h(2)
    op_f(3)
    z_clockwise()
    op_d(4)
    op_g(3)
    op_e(4)
    z_back()
    op_h(3)
    op_f(4)
    back(0)
    op_g(4)
    back(1)
    op_h(4)
    z_rest()
    back(2)
    back(3)
    back(4)

    gate_wide = gate[...].astype(F32)
    up_wide = up[...].astype(F32)
    sig = jax.nn.sigmoid(gate_wide)
    back_grad = bg[...]
    ug[...] = (back_grad * (gate_wide * sig)).astype(BF)
    gg[...] = (back_grad * up_wide * sig * (1.0 + gate_wide * (1.0 - sig))).astype(BF)

    factor = jnp.float32(float(TOK * 32) ** -0.5)
    for n in (2, 4):
        arrived(z2r.at[0, hi_r if n == 2 else lo_r], z_r.at[n])
        arrived(z2r.at[1, lo_r if n == 2 else hi_r], z_r.at[n + 1])
    wg[:, 0:128] = (zf[2] + z2r[0].astype(F32) + z2r[1].astype(F32)) * factor
    arrived(q2r.at[0, c1], z_r.at[8])
    arrived(q2r.at[1, c0], z_r.at[9])
    arrived(q2r.at[0, c0], z_r.at[10])
    arrived(q2r.at[1, c1], z_r.at[11])
    rest = (pr[zh] + q2r[0].astype(F32) + q2r[1].astype(F32)) * factor
    for n in range(4):
        wg[RR * n : RR * n + RR, 128:WIDE] = rest[:, 32 * n : 32 * n + 32]

    for copy in drains:
        copy.wait_send()
    for j in range(NK):
        for side in range(2):
            for t in range(1, NZ):
                @pl.when(line_sends(side, t))
                def _():
                    line_copy(j, side, t).wait_send()


def per_device(out_grad, gate_pre, up_pre, down_weight):
    vmem, dma = pltpu.VMEM, pltpu.SemaphoreType.DMA
    anywhere = pl.BlockSpec(memory_space=pl.ANY)
    local = pl.BlockSpec(memory_space=pltpu.VMEM)
    return pl.pallas_call(
        kernel,
        out_shape=(
            jax.ShapeDtypeStruct((TOK, FFL), BF),
            jax.ShapeDtypeStruct((TOK, FFL), BF),
            jax.ShapeDtypeStruct((FFL, WIDE), F32),
        ),
        in_specs=[local, anywhere, anywhere, anywhere],
        out_specs=(local, local, local),
        scratch_shapes=[
            vmem((TOK, FFL), BF),
            vmem((TOK, FFL), BF),
            vmem((FFL, 4 * QUARTER), BF),
            vmem((4, NK, FFL, 256), BF),
            vmem((FFL, TOK), BF),
            vmem((4, NK, TOK, 256), BF),
            vmem((4, NK, 16, 256), BF),
            vmem((4, NK, 16, 256), BF),
            vmem((TOK, FFL), F32),
            vmem((4, NK, FFL, 128), F32),
            vmem((4, NK, FFL, 128), BF),
            vmem((4, NK, FFL, 128), BF),
            vmem((NK, FFL, 128), BF),
            vmem((NK, FFL, 128), BF),
            vmem((2, NK, FFL, 128), BF),
            vmem((2, NK, FFL, 128), BF),
            vmem((FFL, 128), BF),
            vmem((FFL, 128), BF),
            vmem((2, FFL, 128), BF),
            vmem((2, FFL, 128), BF),
            vmem((3, FFL, 128), F32),
            vmem((4, RR, 128), F32),
            vmem((RR, 128), BF),
            vmem((RR, 128), BF),
            vmem((2, RR, 128), BF),
            vmem((2, RR, 128), BF),
            dma((3,)),
            dma((4,)),
            dma((4,)),
            dma((2, NK, NZ)),
            dma((2, NK, NZ)),
            dma((4, NK)),
            dma((4, NK)),
            dma((4, NK)),
            dma((4, NK)),
            dma((6, NK)),
            dma((6, NK)),
            dma((12,)),
            dma((12,)),
        ],
        compiler_params=pltpu.CompilerParams(
            collective_id=0, has_side_effects=True, vmem_limit_bytes=56 * 2**20
        ),
        cost_estimate=pl.CostEstimate(
            flops=4 * TOK * FFL * 4 * QUARTER, bytes_accessed=7 * 2**20, transcendentals=2 * TOK * FFL
        ),
    )(out_grad, gate_pre, up_pre, down_weight)


def solution(mesh):
    placed = (P(("dp", "tensor"), None), P("dp", "tensor"), P("dp", "tensor"), P("tensor", None))
    return jax.shard_map(
        per_device,
        mesh=mesh,
        in_specs=placed,
        out_specs=(P("dp", "tensor"), P("dp", "tensor"), P("tensor", "dp")),
        check_vma=False,
    )
```

time: 525 us -> 145 us (0.28)
  waiting for transfers between devices: 487 us -> 0 us
  Pallas kernels: 0 us -> 132 us
  matrix products: 14.5 us -> 0 us
  between operations: 14.1 us -> 0.64 us
    reduce_scatter x1 -> x0, waiting for transfers between devices: 253 us -> none  [per_device(): lax.psum_scatter(partial_value.astype(jnp.bfloat16), 'dp', scatter_dimens...]
    all_gather x1 -> x0, waiting for transfers between devices: 233 us -> none  [per_device(): rows_all = lax.all_gather(out_grad, 'tensor', axis=0, tiled=True)]
    pallas_call x0 -> x1, Pallas kernels: none -> 132 us  [per_device(): pl.pallas_call(kernel, out_shape=(jax.ShapeDtypeStruct((TOK, FFL), BF), j...]
    dot_general x2 -> x0, matrix products: 14.5 us -> none  [the longest x1 7.46 us: per_device(): lax.dot_general(hidden, rows_all, (((0,), (0,)), ((), ())), preferred_ele...]
    pallas_call x0 -> x3, local copies, waits for them, and re-layouts: none -> 5.74 us  [per_device(): pl.pallas_call(kernel, out_shape=(jax.ShapeDtypeStruct((TOK, FFL), BF), j...]
  transfers between devices with their start and end apart: 2 -> 0, of which waited for: 2 -> 0; matrix products, arithmetic and copies ran while one was open for 1% -> 0% of each run, Pallas kernels for 0% -> 0%
where the time goes in v1:
time: 145 us; the launch traced here: 142 us
  Pallas kernels  132 us (91%)
  local copies, waits for them, and re-layouts  9.56 us (7%)
    pallas_call x1, Pallas kernels, per_device(): pl.pallas_call(kernel, out_shape=(jax.ShapeDtypeStruct((TOK, FFL), BF), j...  132 us
    pallas_call x3, local copies, waits for them, and re-layouts, per_device(): pl.pallas_call(kernel, out_shape=(jax.ShapeDtypeStruct((TOK, FFL), BF), j...  5.74 us
    unnamed x2, local copies, waits for them, and re-layouts  3.82 us

profile of v1, /device:TPU:1, one launch (start us, length us, event | category | flops | bytes accessed | tf_op | source)
XLA Modules:
  0.0 142.3 jit_solution(14207659601726956496)
XLA Ops:
  0.6 1.9 %copy.7.gate_hbm = bf16[384,448]{1,0:T(8,128)(2,1)} copy(bf16[384,448]{0,1:T(8,128)(2,1)} %param.5) | data formatting | bytes 688128 | tf_op args[1]
  2.5 1.9 %copy.8.up_hbm = bf16[384,448]{1,0:T(8,128)(2,1)} copy(bf16[384,448]{0,1:T(8,128)(2,1)} %param.6) | data formatting | bytes 688128 | tf_op args[2]
  4.4 132.1 %shard_map.67 = (bf16[384,448]{1,0:T(8,128)(2,1)}, bf16[384,448]{1,0:T(8,128)(2,1)}, f32[448,160]{1,0:T(8,128)}) custom-call(bf16[12,5120]{1,0:T(8,128)(2,1)} %og.1, bf16[384,448]{1,0:T(8,128)(2,1)} %copy.7.gate_hbm, bf16[384,448]{1,0:T(8,128)(2,1)} %copy.8.up_hbm, bf16[448,5120]{1,0:T(8,128)(2,1)} %w_hbm.1), custom_call_target="tpu_custom_call" | custom-call | flops 3523215360 | bytes 7340032 | tf_op jit(solution)/shard_map/pallas_call | solution.py:391
  136.5 1.9 %copy.9 = bf16[384,448]{0,1:T(8,128)(2,1)} copy(bf16[384,448]{1,0:T(8,128)(2,1)} %get-tuple-element.3) | data formatting | bytes 688128 | tf_op jit(solution)/shard_map/pallas_call | solution.py:391
  138.4 1.9 %copy.11 = f32[448,160]{0,1:T(8,128)} copy(f32[448,160]{1,0:T(8,128)} %get-tuple-element.5) | data formatting | bytes 573440 | tf_op jit(solution)/shard_map/pallas_call | solution.py:391
  140.4 1.9 %copy.10 = bf16[384,448]{0,1:T(8,128)(2,1)} copy(bf16[384,448]{1,0:T(8,128)(2,1)} %get-tuple-element.4) | data formatting | bytes 688128 | tf_op jit(solution)/shard_map/pallas_call | solution.py:391

commit v2 on v1

--- a/solution.py
+++ b/solution.py
@@ -23,6 +23,7 @@
 WIDE = 160
 R0 = 64
 RR = 112
+NB = 1
 
 
 def tile_columns(load, k):
@@ -42,8 +43,8 @@
     og, gate_hbm, up_hbm, w_hbm,
     gg, ug, wg,
     gate, up, w, wp, ht, xs, asend, arecv, bg, pm, csend, crecv,
-    y1s, y1r, y2s, y2r, z1s, z1r, z2s, z2r, zf, pr, q1s, q1r, q2s, q2r,
-    lsem, a_s, a_r, l_s, l_r, x_s, x_r, c_s, c_r, y_s, y_r, z_s, z_r,
+    ys, yr, z1s, z1r, z2s, z2r, zf, pr, q1s, q1r, q2s, q2r,
+    lsem, a_s, a_r, d_s, d_r, l_s, l_r, b_s, b_r, x_s, x_r, c_s, c_r, y_s, y_r, z_s, z_r,
 ):
     dp = lax.axis_index("dp")
     tn = lax.axis_index("tensor")
@@ -60,7 +61,7 @@
         return (y * 8 + ((zh + d) % 4) * 2 + core, tn)
 
     def at_line(d):
-        return (dp, tn + 4 * d)
+        return (dp, ((zl + d) % NZ) * 4 + x)
 
     other = (dp + 1 - 2 * core, tn)
 
@@ -77,25 +78,29 @@
     def greet(device):
         pl.semaphore_signal(barrier, inc=1, device_id=device, device_id_type=MESH)
 
-    for device in (at_x(1), at_x(2), at_x(3), other, at_y(1), at_y(3), at_z(1), at_z(3)):
+    for d in (1, 2, 3):
+        greet(at_x(d))
+        greet(at_y(d))
+    for device in (other, at_z(1), at_z(3)):
         greet(device)
-
-    @pl.when(zl > 0)
-    def _():
-        greet(at_line(-1))
-
-    @pl.when(zl < NZ - 1)
-    def _():
-        greet(at_line(1))
+    for d in range(1, NZ):
+        greet(at_line(d))
+
+    def slot(k):
+        if k == 4:
+            return 3
+        ahead = (k + 4 - zh) % 4
+        return jnp.where(ahead == 2, 0, jnp.where(ahead == 1, 1, jnp.where(ahead == 3, 2, 4)))
+
+    order = [(zh + 2) % 4, (zh + 1) % 4, (zh + 3) % 4, 4, zh]
 
     asend[...] = jnp.zeros_like(asend)
     for q in range(4):
         for k in range(NK):
             lo, hi = tile_columns(lambda at, n: og[:, q * QUARTER + at : q * QUARTER + at + n], k)
-            asend[q, k, 0:OWN, 0:128] = lo
-            asend[q, k, 0:OWN, 128:256] = hi
-    inner = jnp.where(zl > 0, 1, 0) + jnp.where(zl < NZ - 1, 1, 0)
-    pl.semaphore_wait(barrier, 8 + inner)
+            asend[q, slot(k), 0:OWN, 0:128] = lo
+            asend[q, slot(k), 0:OWN, 128:256] = hi
+    pl.semaphore_wait(barrier, 9 + NZ - 1)
 
     drains = []
 
@@ -112,26 +117,37 @@
     def arrived(dst, rs):
         remote(dst, dst, rs, rs, other).wait_recv()
 
-    for d in (2, 1, 3):
-        send(asend.at[(x + d) % 4], arecv.at[x], a_s.at[d], a_r.at[d], at_x(d))
-    arecv[pl.ds(x, 1)] = asend[pl.ds(x, 1)]
-
-    loads[0].wait()
-    loads[1].wait()
-    g = gate[...].astype(F32)
-    hidden = (g * jax.nn.sigmoid(g) * up[...].astype(F32)).astype(BF)
-    ht[...] = hidden.T
-    for d in (1, 3, 2):
-        arrived(arecv.at[(x + 4 - d) % 4], a_r.at[d])
-
-    order = [(zh + 2) % 4, (zh + 1) % 4, (zh + 3) % 4, 4, zh]
-
     def rows_of(p):
         return pl.ds(pl.multiple_of(p * LINE, 16), LINE)
 
-    for j in range(NK):
-        mine = jnp.concatenate([arecv[s, order[j], 0:OWN, :] for s in range(4)], axis=0)
+    later = pl.ds(1, NK - 1)
+
+    for d in (2, 1, 3):
+        send(asend.at[(x + d) % 4, 0], arecv.at[x, 0], a_s.at[0, d], a_r.at[0, d], at_x(d))
+    for d in (2, 1, 3):
+        send(asend.at[(x + d) % 4, later], arecv.at[x, later], a_s.at[1, d], a_r.at[1, d], at_x(d))
+    arecv[pl.ds(x, 1)] = asend[pl.ds(x, 1)]
+
+    def own_rows(j):
+        mine = jnp.concatenate([arecv[n, j, 0:OWN, :] for n in range(4)], axis=0)
         xs[x, j, rows_of(zl), :] = mine
+
+    def to_ring(j, p):
+        block = xs.at[x, j, rows_of(p)]
+        for d in (2, 1, 3):
+            remote(block, block, b_s.at[j, d], b_r.at[j, d], at_x(d)).start()
+
+    for d in (1, 3, 2):
+        arrived(arecv.at[(x + 4 - d) % 4, 0], a_r.at[0, d])
+    own_rows(0)
+    block = xs.at[x, 0, rows_of(zl)]
+    for d in (4, 3, 5, 2, 6, 1, 7):
+        remote(block, block, d_s.at[0], d_r.at[zl], at_line(d)).start()
+    to_ring(0, zl)
+    for d in (1, 3, 2):
+        arrived(arecv.at[(x + 4 - d) % 4, later], a_r.at[1, d])
+    for j in range(1, NK):
+        own_rows(j)
 
     def line_copy(j, side, t):
         step = 1 if side == 0 else -1
@@ -146,22 +162,45 @@
     def line_gets(side, t):
         return zl - t >= 0 if side == 0 else zl + t <= NZ - 1
 
-    def wave(w_at):
-        for j in range(NK):
-            t = w_at - 2 * j
-            if t < 0 or t > NZ - 1:
-                continue
+    def wave(t):
+        for j in range(1, NK):
             for side in range(2):
+                step = 1 if side == 0 else -1
                 if t >= 1:
+
                     @pl.when(line_gets(side, t))
                     def _():
-                        step = 1 if side == 0 else -1
                         arrived(xs.at[x, j, rows_of(zl - step * t)], l_r.at[side, j, t])
 
                 if t + 1 <= NZ - 1:
+
                     @pl.when(line_sends(side, t + 1))
                     def _():
                         line_copy(j, side, t + 1).start()
+
+                if t >= 1 and j <= NB:
+
+                    @pl.when(line_gets(side, t))
+                    def _():
+                        to_ring(j, zl - step * t)
+
+            if t == 0 and j <= NB:
+                to_ring(j, zl)
+
+    def direct(t):
+        for side in range(2):
+            step = 1 if side == 0 else -1
+
+            @pl.when(line_gets(side, t))
+            def _():
+                p = zl - step * t
+                arrived(xs.at[x, 0, rows_of(p)], d_r.at[p])
+                to_ring(0, p)
+
+    def ring_in(j, d):
+        q = (x + 4 - d) % 4
+        arrived(xs.at[q, j], b_r.at[j, d])
+        partial(q, j)
 
     def permute(q):
         if q == 0:
@@ -203,39 +242,21 @@
         partial(far, j)
 
     lo_r, hi_r = pl.ds(0, HALF), pl.ds(HALF, HALF)
-    y_far, y_next, y_prev = (y + 2) % 4, (y + 1) % 4, (y + 3) % 4
 
     def op_f(j):
         for q in range(4):
             arrived(crecv.at[q, j], c_r.at[q, j])
-        y1s[j] = (pm[y_far, j] + crecv[y_far, j].astype(F32)).astype(BF)
-        send(y1s.at[j, lo_r], y1r.at[j, lo_r], y_s.at[0, j], y_r.at[0, j], at_y(1))
-        send(y1s.at[j, hi_r], y1r.at[j, hi_r], y_s.at[1, j], y_r.at[1, j], at_y(3))
-        y2s[0, j, hi_r] = (pm[y_next, j, hi_r] + crecv[y_next, j, hi_r].astype(F32)).astype(BF)
-        send(y2s.at[0, j, hi_r], y2r.at[0, j, hi_r], y_s.at[2, j], y_r.at[2, j], at_y(1))
-        y2s[1, j, lo_r] = (pm[y_prev, j, lo_r] + crecv[y_prev, j, lo_r].astype(F32)).astype(BF)
-        send(y2s.at[1, j, lo_r], y2r.at[1, j, lo_r], y_s.at[3, j], y_r.at[3, j], at_y(3))
-
-    def op_g(j):
-        arrived(y1r.at[j, lo_r], y_r.at[0, j])
-        y2s[0, j, lo_r] = (
-            pm[y_next, j, lo_r] + crecv[y_next, j, lo_r].astype(F32) + y1r[j, lo_r].astype(F32)
-        ).astype(BF)
-        send(y2s.at[0, j, lo_r], y2r.at[0, j, lo_r], y_s.at[4, j], y_r.at[4, j], at_y(1))
-        arrived(y1r.at[j, hi_r], y_r.at[1, j])
-        y2s[1, j, hi_r] = (
-            pm[y_prev, j, hi_r] + crecv[y_prev, j, hi_r].astype(F32) + y1r[j, hi_r].astype(F32)
-        ).astype(BF)
-        send(y2s.at[1, j, hi_r], y2r.at[1, j, hi_r], y_s.at[5, j], y_r.at[5, j], at_y(3))
+        for d in (2, 1, 3):
+            q = (y + d) % 4
+            ys[d - 1, j] = (pm[q, j] + crecv[q, j].astype(F32)).astype(BF)
+            send(ys.at[d - 1, j], yr.at[d - 1, j], y_s.at[d - 1, j], y_r.at[d - 1, j], at_y(d))
 
     def reduced(j):
-        arrived(y2r.at[0, j, hi_r], y_r.at[2, j])
-        arrived(y2r.at[1, j, lo_r], y_r.at[3, j])
-        arrived(y2r.at[0, j, lo_r], y_r.at[4, j])
-        arrived(y2r.at[1, j, hi_r], y_r.at[5, j])
-        return (
-            pm[y, j] + crecv[y, j].astype(F32) + y2r[0, j].astype(F32) + y2r[1, j].astype(F32)
-        )
+        total = pm[y, j] + crecv[y, j].astype(F32)
+        for d in (1, 3, 2):
+            arrived(yr.at[d - 1, j], y_r.at[d - 1, j])
+            total = total + yr[d - 1, j].astype(F32)
+        return total
 
     z_far, z_next, z_prev = (zh + 2) % 4, (zh + 1) % 4, (zh + 3) % 4
 
@@ -292,7 +313,7 @@
         value = None
         for q in range(4):
             term = lax.dot_general(
-                xs[q, j], wp[q, order[j]], (((1,), (1,)), ((), ())), preferred_element_type=F32
+                wp[q, order[j]], xs[q, j], (((1,), (1,)), ((), ())), preferred_element_type=F32
             )
             value = term if value is None else value + term
         if j == 0:
@@ -301,55 +322,60 @@
             bg[...] += value
 
     wave(0)
-    for n in range(4):
-        wave(n + 1)
-        permute(n)
+    loads[0].wait()
+    loads[1].wait()
+    g = gate[...].astype(F32)
+    ht[...] = (g * jax.nn.sigmoid(g) * up[...].astype(F32)).astype(BF)
+    direct(1)
+    direct(2)
+    wave(1)
+    direct(3)
+    direct(4)
+    wave(2)
+    direct(5)
+    direct(6)
+    direct(7)
+    wave(3)
+    partial(x, 0)
+    wave(4)
+    ring_in(0, 1)
+    ring_in(0, 3)
     wave(5)
+    ring_in(0, 2)
     wave(6)
+    op_f(0)
     wave(7)
-    op_a(0)
-    wave(8)
-    wave(9)
-    wave(10)
-    op_d(0)
-    op_a(1)
-    wave(11)
     op_a(2)
-    wave(12)
-    op_e(0)
-    wave(13)
-    op_f(0)
-    op_d(1)
-    wave(14)
+    partial(x, 1)
+    ring_in(1, 1)
+    ring_in(1, 3)
     op_a(3)
-    op_g(0)
-    wave(15)
-    op_e(1)
+    ring_in(1, 2)
     op_h(0)
     op_f(1)
     op_d(2)
     op_a(4)
-    op_g(1)
     op_e(2)
     op_h(1)
     op_f(2)
     op_d(3)
-    op_g(2)
     op_e(3)
     op_h(2)
     op_f(3)
     z_clockwise()
+    z_back()
     op_d(4)
-    op_g(3)
+    op_h(3)
     op_e(4)
-    z_back()
-    op_h(3)
     op_f(4)
+    permute(0)
+    permute(1)
+    z_rest()
+    op_h(4)
+    permute(2)
+    permute(3)
     back(0)
-    op_g(4)
     back(1)
-    op_h(4)
-    z_rest()
     back(2)
     back(3)
     back(4)
@@ -365,20 +391,25 @@
     for n in (2, 4):
         arrived(z2r.at[0, hi_r if n == 2 else lo_r], z_r.at[n])
         arrived(z2r.at[1, lo_r if n == 2 else hi_r], z_r.at[n + 1])
-    wg[:, 0:128] = (zf[2] + z2r[0].astype(F32) + z2r[1].astype(F32)) * factor
+    wg[0:128] = ((zf[2] + z2r[0].astype(F32) + z2r[1].astype(F32)) * factor).T
     arrived(q2r.at[0, c1], z_r.at[8])
     arrived(q2r.at[1, c0], z_r.at[9])
     arrived(q2r.at[0, c0], z_r.at[10])
     arrived(q2r.at[1, c1], z_r.at[11])
-    rest = (pr[zh] + q2r[0].astype(F32) + q2r[1].astype(F32)) * factor
-    for n in range(4):
-        wg[RR * n : RR * n + RR, 128:WIDE] = rest[:, 32 * n : 32 * n + 32]
+    rest = ((pr[zh] + q2r[0].astype(F32) + q2r[1].astype(F32)) * factor).T
+    wg[128:WIDE] = jnp.concatenate([rest[32 * n : 32 * n + 32] for n in range(4)], axis=1)
 
     for copy in drains:
         copy.wait_send()
-    for j in range(NK):
+    others = xs.at[0, 0, pl.ds(0, (NZ - 1) * LINE)]
+    remote(others, others, d_s.at[0], d_s.at[0], other).wait_send()
+    for j in range(NB + 1):
+        for d in (1, 2, 3):
+            remote(xs.at[x, j], xs.at[x, j], b_s.at[j, d], b_s.at[j, d], other).wait_send()
+    for j in range(1, NK):
         for side in range(2):
             for t in range(1, NZ):
+
                 @pl.when(line_sends(side, t))
                 def _():
                     line_copy(j, side, t).wait_send()
@@ -388,32 +419,30 @@
     vmem, dma = pltpu.VMEM, pltpu.SemaphoreType.DMA
     anywhere = pl.BlockSpec(memory_space=pl.ANY)
     local = pl.BlockSpec(memory_space=pltpu.VMEM)
-    return pl.pallas_call(
+    gate_grad, up_grad, weight_grad = pl.pallas_call(
         kernel,
         out_shape=(
-            jax.ShapeDtypeStruct((TOK, FFL), BF),
-            jax.ShapeDtypeStruct((TOK, FFL), BF),
-            jax.ShapeDtypeStruct((FFL, WIDE), F32),
+            jax.ShapeDtypeStruct((FFL, TOK), BF),
+            jax.ShapeDtypeStruct((FFL, TOK), BF),
+            jax.ShapeDtypeStruct((WIDE, FFL), F32),
         ),
         in_specs=[local, anywhere, anywhere, anywhere],
         out_specs=(local, local, local),
         scratch_shapes=[
-            vmem((TOK, FFL), BF),
-            vmem((TOK, FFL), BF),
+            vmem((FFL, TOK), BF),
+            vmem((FFL, TOK), BF),
             vmem((FFL, 4 * QUARTER), BF),
             vmem((4, NK, FFL, 256), BF),
             vmem((FFL, TOK), BF),
             vmem((4, NK, TOK, 256), BF),
             vmem((4, NK, 16, 256), BF),
             vmem((4, NK, 16, 256), BF),
-            vmem((TOK, FFL), F32),
+            vmem((FFL, TOK), F32),
             vmem((4, NK, FFL, 128), F32),
             vmem((4, NK, FFL, 128), BF),
             vmem((4, NK, FFL, 128), BF),
-            vmem((NK, FFL, 128), BF),
-            vmem((NK, FFL, 128), BF),
-            vmem((2, NK, FFL, 128), BF),
-            vmem((2, NK, FFL, 128), BF),
+            vmem((3, NK, FFL, 128), BF),
+            vmem((3, NK, FFL, 128), BF),
             vmem((FFL, 128), BF),
             vmem((FFL, 128), BF),
             vmem((2, FFL, 128), BF),
@@ -425,16 +454,20 @@
             vmem((2, RR, 128), BF),
             vmem((2, RR, 128), BF),
             dma((3,)),
-            dma((4,)),
-            dma((4,)),
+            dma((2, 4)),
+            dma((2, 4)),
+            dma((1,)),
+            dma((NZ,)),
             dma((2, NK, NZ)),
             dma((2, NK, NZ)),
+            dma((NB + 1, 4)),
+            dma((NB + 1, 4)),
             dma((4, NK)),
             dma((4, NK)),
             dma((4, NK)),
             dma((4, NK)),
-            dma((6, NK)),
-            dma((6, NK)),
+            dma((3, NK)),
+            dma((3, NK)),
             dma((12,)),
             dma((12,)),
         ],
@@ -444,7 +477,8 @@
         cost_estimate=pl.CostEstimate(
             flops=4 * TOK * FFL * 4 * QUARTER, bytes_accessed=7 * 2**20, transcendentals=2 * TOK * FFL
         ),
-    )(out_grad, gate_pre, up_pre, down_weight)
+    )(out_grad, gate_pre.T, up_pre.T, down_weight)
+    return gate_grad.T, up_grad.T, weight_grad.T
 
 
 def solution(mesh):

time: 145 us -> 126 us (0.87); the launches traced: 142 us -> 125 us
  Pallas kernels: 132 us -> 119 us
  local copies, waits for them, and re-layouts: 9.56 us -> 5.2 us
    pallas_call x1, Pallas kernels: 132 us -> 119 us  [per_device(): pl.pallas_call(kernel, out_shape=(jax.ShapeDtypeStruct((FFL, TOK), BF), j...]
    pallas_call x3 -> x0, local copies, waits for them, and re-layouts: 5.74 us -> none  [per_device(): pl.pallas_call(kernel, out_shape=(jax.ShapeDtypeStruct((TOK, FFL), BF), j...]
    unnamed x2 -> x3, local copies, waits for them, and re-layouts: 3.82 us -> 5.2 us
where the time goes in v2:
time: 126 us; the launch traced here: 125 us
  Pallas kernels  119 us (94%)
  local copies, waits for them, and re-layouts  5.2 us (4%)
    pallas_call x1, Pallas kernels, per_device(): pl.pallas_call(kernel, out_shape=(jax.ShapeDtypeStruct((FFL, TOK), BF), j...  119 us
    unnamed x3, local copies, waits for them, and re-layouts  5.2 us

profile of v2, /device:TPU:1, one launch (start us, length us, event | category | flops | bytes accessed | tf_op | source)
XLA Modules:
  0.0 125.3 jit_solution(14343655368848025255)
XLA Ops:
  0.6 119.4 %shard_map.67 = (bf16[448,384]{1,0:T(8,128)(2,1)}, bf16[448,384]{1,0:T(8,128)(2,1)}, f32[160,448]{1,0:T(8,128)}) custom-call(bf16[12,5120]{1,0:T(8,128)(2,1)} %og.1, bf16[448,384]{1,0:T(8,128)(2,1)} %bitcast.8, bf16[448,384]{1,0:T(8,128)(2,1)} %bitcast.9, bf16[448,5120]{1,0:T(8,128)(2,1)} %w_hbm.1), custom_call_target="tpu_custom_call" | custom-call | flops 3523215360 | bytes 7340032 | tf_op jit(solution)/shard_map/pallas_call | solution.py:422
  120.1 1.7 %copy.10 = bf16[384,448]{0,1:T(8,128)(2,1)} copy(bf16[384,448]{0,1:T(8,128)(2,1)} %bitcast.6) | data formatting | bytes 688128
  121.8 1.7 %copy.11 = bf16[384,448]{0,1:T(8,128)(2,1)} copy(bf16[384,448]{0,1:T(8,128)(2,1)} %bitcast.5) | data formatting | bytes 688128
  123.6 1.7 %copy.12 = f32[448,160]{0,1:T(8,128)} copy(f32[448,160]{0,1:T(8,128)} %bitcast.7) | data formatting | bytes 573440

commit v3 on v2

--- a/solution.py
+++ b/solution.py
@@ -23,7 +23,8 @@
 WIDE = 160
 R0 = 64
 RR = 112
-NB = 1
+NB = 2
+NS = 2
 
 
 def tile_columns(load, k):
@@ -134,8 +135,12 @@
 
     def to_ring(j, p):
         block = xs.at[x, j, rows_of(p)]
-        for d in (2, 1, 3):
-            remote(block, block, b_s.at[j, d], b_r.at[j, d], at_x(d)).start()
+        if j == 0:
+            for d in (2, 1, 3):
+                remote(block, block, b_s.at[d], b_r.at[d], at_x(d)).start()
+        else:
+            remote(block, block, x_s.at[0, j], x_r.at[0, j], at_x(1)).start()
+            remote(block, block, x_s.at[1, j], x_r.at[1, j], at_x(3)).start()
 
     for d in (1, 3, 2):
         arrived(arecv.at[(x + 4 - d) % 4, 0], a_r.at[0, d])
@@ -151,41 +156,63 @@
 
     def line_copy(j, side, t):
         step = 1 if side == 0 else -1
-        block = xs.at[x, j, rows_of(zl - step * (t - 1))]
-        return remote(block, block, l_s.at[side, j, t], l_r.at[side, j, t], at_line(step))
-
-    def line_sends(side, t):
+        back, far = ((t - 1) // 2 * 2, 2 - t % 2) if j <= NS else (t - 1, 1)
+        block = xs.at[x, j, rows_of(zl - step * back)]
+        return remote(block, block, l_s.at[side, j, t], l_r.at[side, j, t], at_line(step * far))
+
+    def line_sends(j, side, t):
+        back, far = ((t - 1) // 2 * 2, 2 - t % 2) if j <= NS else (t - 1, 1)
         if side == 0:
-            return jnp.logical_and(zl - (t - 1) >= 0, zl < NZ - 1)
-        return jnp.logical_and(zl + (t - 1) <= NZ - 1, zl > 0)
+            return jnp.logical_and(zl - back >= 0, zl + far <= NZ - 1)
+        return jnp.logical_and(zl + back <= NZ - 1, zl - far >= 0)
 
     def line_gets(side, t):
         return zl - t >= 0 if side == 0 else zl + t <= NZ - 1
 
+    def line_send(j, side, t):
+        @pl.when(line_sends(j, side, t))
+        def _():
+            line_copy(j, side, t).start()
+
+    def line_get(j, side, t):
+        step = 1 if side == 0 else -1
+
+        @pl.when(line_gets(side, t))
+        def _():
+            arrived(xs.at[x, j, rows_of(zl - step * t)], l_r.at[side, j, t])
+
+    def line_ring(j, side, t):
+        step = 1 if side == 0 else -1
+
+        @pl.when(line_gets(side, t))
+        def _():
+            to_ring(j, zl - step * t)
+
     def wave(t):
         for j in range(1, NK):
-            for side in range(2):
-                step = 1 if side == 0 else -1
-                if t >= 1:
-
-                    @pl.when(line_gets(side, t))
-                    def _():
-                        arrived(xs.at[x, j, rows_of(zl - step * t)], l_r.at[side, j, t])
-
-                if t + 1 <= NZ - 1:
-
-                    @pl.when(line_sends(side, t + 1))
-                    def _():
-                        line_copy(j, side, t + 1).start()
-
-                if t >= 1 and j <= NB:
-
-                    @pl.when(line_gets(side, t))
-                    def _():
-                        to_ring(j, zl - step * t)
-
-            if t == 0 and j <= NB:
-                to_ring(j, zl)
+            if j <= NS:
+                if t > 4:
+                    continue
+                arrivals = [n for n in (2 * t, 2 * t - 1) if 1 <= n <= NZ - 1]
+                relay, leave = 2 * t, [n for n in (2 * t + 2, 2 * t + 1) if n <= NZ - 1]
+            else:
+                arrivals = [t] if t >= 1 else []
+                relay, leave = t, [t + 1] if t + 1 <= NZ - 1 else []
+            for n in arrivals:
+                for side in range(2):
+                    line_get(j, side, n)
+                    if n == relay:
+                        for m in leave:
+                            line_send(j, side, m)
+                if j <= NB:
+                    for side in range(2):
+                        line_ring(j, side, n)
+            if t == 0:
+                for m in leave:
+                    for side in range(2):
+                        line_send(j, side, m)
+                if j <= NB:
+                    to_ring(j, zl)
 
     def direct(t):
         for side in range(2):
@@ -197,10 +224,10 @@
                 arrived(xs.at[x, 0, rows_of(p)], d_r.at[p])
                 to_ring(0, p)
 
-    def ring_in(j, d):
+    def ring_in(d):
         q = (x + 4 - d) % 4
-        arrived(xs.at[q, j], b_r.at[j, d])
-        partial(q, j)
+        arrived(xs.at[q, 0], b_r.at[d])
+        partial(q, 0)
 
     def permute(q):
         if q == 0:
@@ -331,38 +358,37 @@
     wave(1)
     direct(3)
     direct(4)
+    direct(5)
     wave(2)
-    direct(5)
     direct(6)
     direct(7)
+    partial(x, 0)
     wave(3)
-    partial(x, 0)
+    ring_in(1)
+    ring_in(3)
     wave(4)
-    ring_in(0, 1)
-    ring_in(0, 3)
+    partial(x, 1)
+    ring_in(2)
+    op_f(0)
     wave(5)
-    ring_in(0, 2)
+    op_d(1)
     wave(6)
-    op_f(0)
+    partial(x, 2)
+    op_d(2)
     wave(7)
-    op_a(2)
-    partial(x, 1)
-    ring_in(1, 1)
-    ring_in(1, 3)
     op_a(3)
-    ring_in(1, 2)
+    op_e(1)
+    op_a(4)
     op_h(0)
     op_f(1)
-    op_d(2)
-    op_a(4)
     op_e(2)
+    op_f(2)
     op_h(1)
-    op_f(2)
     op_d(3)
+    op_h(2)
     op_e(3)
-    op_h(2)
+    z_clockwise()
     op_f(3)
-    z_clockwise()
     z_back()
     op_d(4)
     op_h(3)
@@ -370,8 +396,8 @@
     op_f(4)
     permute(0)
     permute(1)
+    op_h(4)
     z_rest()
-    op_h(4)
     permute(2)
     permute(3)
     back(0)
@@ -403,29 +429,39 @@
         copy.wait_send()
     others = xs.at[0, 0, pl.ds(0, (NZ - 1) * LINE)]
     remote(others, others, d_s.at[0], d_s.at[0], other).wait_send()
-    for j in range(NB + 1):
-        for d in (1, 2, 3):
-            remote(xs.at[x, j], xs.at[x, j], b_s.at[j, d], b_s.at[j, d], other).wait_send()
+    whole = xs.at[x, 0]
+    for d in (1, 2, 3):
+        remote(whole, whole, b_s.at[d], b_s.at[d], other).wait_send()
+    for j in range(1, NB + 1):
+        for n in (0, 1):
+            remote(whole, whole, x_s.at[n, j], x_s.at[n, j], other).wait_send()
     for j in range(1, NK):
         for side in range(2):
             for t in range(1, NZ):
 
-                @pl.when(line_sends(side, t))
+                @pl.when(line_sends(j, side, t))
                 def _():
                     line_copy(j, side, t).wait_send()
+
+
+def write_out(a, b, c, a_out, b_out, c_out):
+    a_out[...] = a[...]
+    b_out[...] = b[...]
+    c_out[...] = c[...]
 
 
 def per_device(out_grad, gate_pre, up_pre, down_weight):
     vmem, dma = pltpu.VMEM, pltpu.SemaphoreType.DMA
     anywhere = pl.BlockSpec(memory_space=pl.ANY)
     local = pl.BlockSpec(memory_space=pltpu.VMEM)
-    gate_grad, up_grad, weight_grad = pl.pallas_call(
+    sizes = (
+        jax.ShapeDtypeStruct((FFL, TOK), BF),
+        jax.ShapeDtypeStruct((FFL, TOK), BF),
+        jax.ShapeDtypeStruct((WIDE, FFL), F32),
+    )
+    parts = pl.pallas_call(
         kernel,
-        out_shape=(
-            jax.ShapeDtypeStruct((FFL, TOK), BF),
-            jax.ShapeDtypeStruct((FFL, TOK), BF),
-            jax.ShapeDtypeStruct((WIDE, FFL), F32),
-        ),
+        out_shape=sizes,
         in_specs=[local, anywhere, anywhere, anywhere],
         out_specs=(local, local, local),
         scratch_shapes=[
@@ -460,8 +496,8 @@
             dma((NZ,)),
             dma((2, NK, NZ)),
             dma((2, NK, NZ)),
-            dma((NB + 1, 4)),
-            dma((NB + 1, 4)),
+            dma((4,)),
+            dma((4,)),
             dma((4, NK)),
             dma((4, NK)),
             dma((4, NK)),
@@ -478,6 +514,12 @@
             flops=4 * TOK * FFL * 4 * QUARTER, bytes_accessed=7 * 2**20, transcendentals=2 * TOK * FFL
         ),
     )(out_grad, gate_pre.T, up_pre.T, down_weight)
+    gate_grad, up_grad, weight_grad = pl.pallas_call(
+        write_out,
+        out_shape=sizes,
+        in_specs=[local] * 3,
+        out_specs=(local,) * 3,
+    )(*parts)
     return gate_grad.T, up_grad.T, weight_grad.T
 
 

time: 126 us -> 120 us (0.952)
  local copies, waits for them, and re-layouts: 5.2 us -> 0 us
    unnamed x3 -> x0, local copies, waits for them, and re-layouts: 5.2 us -> none
    pallas_call x1 -> x2, Pallas kernels: 119 us -> 119 us  [the longest x1 117 us: per_device(): pl.pallas_call(kernel, out_shape=sizes, in_specs=[local, anywhere, anywhe...]
where the time goes in v3:
time: 120 us
  Pallas kernels  119 us (99%)
    pallas_call x1, Pallas kernels, per_device(): pl.pallas_call(kernel, out_shape=sizes, in_specs=[local, anywhere, anywhe...  117 us

profile of v3, /device:TPU:1, one launch (start us, length us, event | category | flops | bytes accessed | tf_op | source)
XLA Modules:
  0.0 119.9 jit_solution(3729527618553378292)
XLA Ops:
  0.6 117.1 %shard_map.67 = (bf16[448,384]{1,0:T(8,128)(2,1)}, bf16[448,384]{1,0:T(8,128)(2,1)}, f32[160,448]{1,0:T(8,128)}) custom-call(bf16[12,5120]{1,0:T(8,128)(2,1)} %og.1, bf16[448,384]{1,0:T(8,128)(2,1)} %bitcast.5, bf16[448,384]{1,0:T(8,128)(2,1)} %bitcast.6, bf16[448,5120]{1,0:T(8,128)(2,1)} %w_hbm.1), custom_call_target="tpu_custom_call" | custom-call | flops 3523215360 | bytes 7340032 | tf_op jit(solution)/shard_map/pallas_call | solution.py:462
  117.7 2.2 %shard_map.68 = (bf16[448,384]{1,0:T(8,128)(2,1)}, bf16[448,384]{1,0:T(8,128)(2,1)}, f32[160,448]{1,0:T(8,128)}) custom-call(bf16[448,384]{1,0:T(8,128)(2,1)} %get-tuple-element.9.a, bf16[448,384]{1,0:T(8,128)(2,1)} %get-tuple-element.10.b, f32[160,448]{1,0:T(8,128)} %get-tuple-element.11.c), custom_call_target="tpu_custom_call" | custom-call | tf_op jit(solution)/shard_map/pallas_call | solution.py:517

commit v4 on v3

--- a/solution.py
+++ b/solution.py
@@ -248,18 +248,21 @@
     up_half, down_half = pl.ds(0, TOK // 2), pl.ds(TOK // 2, TOK // 2)
 
     def op_a(j):
-        block = xs.at[x, j]
-        send(block, block, x_s.at[0, j], x_r.at[0, j], at_x(1))
-        send(block, block, x_s.at[1, j], x_r.at[1, j], at_x(3))
+        for n, half, d in ((0, up_half, 1), (1, down_half, 3), (4, down_half, 1), (5, up_half, 3)):
+            block = xs.at[x, j, half]
+            send(block, block, x_s.at[n, j], x_r.at[n, j], at_x(d))
         partial(x, j)
 
     def op_d(j):
-        arrived(xs.at[left, j], x_r.at[0, j])
+        arrived(xs.at[left, j] if j <= NB else xs.at[left, j, up_half], x_r.at[0, j])
         block = xs.at[left, j, up_half]
         send(block, block, x_s.at[2, j], x_r.at[2, j], at_x(1))
-        arrived(xs.at[right, j], x_r.at[1, j])
+        arrived(xs.at[right, j] if j <= NB else xs.at[right, j, down_half], x_r.at[1, j])
         block = xs.at[right, j, down_half]
         send(block, block, x_s.at[3, j], x_r.at[3, j], at_x(3))
+        if j > NB:
+            arrived(xs.at[left, j, down_half], x_r.at[4, j])
+            arrived(xs.at[right, j, up_half], x_r.at[5, j])
         partial(left, j)
         partial(right, j)
 
@@ -498,8 +501,8 @@
             dma((2, NK, NZ)),
             dma((4,)),
             dma((4,)),
-            dma((4, NK)),
-            dma((4, NK)),
+            dma((6, NK)),
+            dma((6, NK)),
             dma((4, NK)),
             dma((4, NK)),
             dma((3, NK)),

time: 120 us -> 120 us (level)
  no operation moved by 1% of the time
where the time goes in v4:
time: 120 us
  Pallas kernels  119 us (99%)
    pallas_call x1, Pallas kernels, per_device(): pl.pallas_call(kernel, out_shape=sizes, in_specs=[local, anywhere, anywhe...  117 us

profile of v4, /device:TPU:1, one launch (start us, length us, event | category | flops | bytes accessed | tf_op | source)
XLA Modules:
  0.0 120.1 jit_solution(14869840926711319244)
XLA Ops:
  0.6 117.3 %shard_map.67 = (bf16[448,384]{1,0:T(8,128)(2,1)}, bf16[448,384]{1,0:T(8,128)(2,1)}, f32[160,448]{1,0:T(8,128)}) custom-call(bf16[12,5120]{1,0:T(8,128)(2,1)} %og.1, bf16[448,384]{1,0:T(8,128)(2,1)} %bitcast.5, bf16[448,384]{1,0:T(8,128)(2,1)} %bitcast.6, bf16[448,5120]{1,0:T(8,128)(2,1)} %w_hbm.1), custom_call_target="tpu_custom_call" | custom-call | flops 3523215360 | bytes 7340032 | tf_op jit(solution)/shard_map/pallas_call | solution.py:465
  117.9 2.2 %shard_map.68 = (bf16[448,384]{1,0:T(8,128)(2,1)}, bf16[448,384]{1,0:T(8,128)(2,1)}, f32[160,448]{1,0:T(8,128)}) custom-call(bf16[448,384]{1,0:T(8,128)(2,1)} %get-tuple-element.9.a, bf16[448,384]{1,0:T(8,128)(2,1)} %get-tuple-element.10.b, f32[160,448]{1,0:T(8,128)} %get-tuple-element.11.c), custom_call_target="tpu_custom_call" | custom-call | tf_op jit(solution)/shard_map/pallas_call | solution.py:520
